TPU v7x, 256 devices: a whole 4x4x8 slice. The times are simulated.
256 devices in a mesh: row: 16 (over y, x_hi, core), col: 16 (over x_lo, z).
Axes of the slice: x: 4 (x_hi: 2, x_lo: 2; x = x_hi * 2 + x_lo), y: 4, z: 8, core: 2. Of those that a mesh axis runs over, the one named last changes fastest.
Arguments:
- pair_state: bfloat16 [768, 768, 128], P('row', 'col'), may hold values from -6 to 6
- residue_mask: int32 [768], replicated, may hold values 0 or 1
- weight_in: bfloat16 [2, 128, 4, 128], replicated, may hold values from -0.5 to 0.5
- weight_gate: bfloat16 [2, 128, 128], replicated, may hold values from -0.5 to 0.5
- weight_out: bfloat16 [2, 128, 128], replicated, may hold values from -0.5 to 0.5
- gain_in: float32 [2, 128], replicated, may hold values from 0.25 to 1.75
- gain_out: float32 [2, 128], replicated, may hold values from 0.25 to 1.75
Outputs:
- updated: bfloat16 [768, 768, 128], P('row', 'col')
Inputs may be any that keep to these rules, and one draw needn't show every extreme that they name: `residue_mask`: 1 marks a residue present in the crop, 0 a padded one.
All inputs are finite; a program needn't handle non-finite values.
Results may differ from a plain program's by a relative error of at most 0.0095.
Values may be sent and summed in bfloat16 or wider, within the bound.
A program may use at most 128 MiB of HBM per device.

v0:
```python
import jax
import jax.numpy as jnp
from jax import lax
from jax.experimental import pallas as pl
from jax.experimental.pallas import tpu as pltpu
from jax.sharding import PartitionSpec as P

MESH = pl.DeviceIdType.MESH
F32 = jnp.float32
BF16 = jnp.bfloat16
EPS = 1e-5
COLS_OUT, ROWS_OUT, PAIR_RIGHT, PAIR_LEFT, ROWS_BACK, COLS_BACK = range(6)


def sigmoid(x):
    return 0.5 * jnp.tanh(0.5 * x) + 0.5


def norm_rows(values, gain):
    mean = jnp.sum(values, axis=0, keepdims=True) * (1.0 / 128.0)
    centered = values - mean
    var = jnp.sum(centered * centered, axis=0, keepdims=True) * (1.0 / 128.0)
    return (centered * lax.rsqrt(var + EPS) * gain).astype(BF16)


def nn(a, b):
    return lax.dot_general(a, b, (((1,), (0,)), ((), ())), preferred_element_type=F32)


def nt(a, b):
    return lax.dot_general(a, b, (((1,), (1,)), ((), ())), preferred_element_type=F32)


def tn(a, b):
    return lax.dot_general(a, b, (((0,), (0,)), ((), ())), preferred_element_type=F32)


def loop(n, body, start=0):
    def step(i, carry):
        body(i)
        return carry

    lax.fori_loop(start, n, step, 0)


def wait_bytes(ref, sem):
    pltpu.make_async_copy(ref, ref, sem).wait()


def kernel(
    x_ref, mask_ref, win_ref, wgate_ref, wout_ref, gin_ref, gout_ref, out_ref,
    perm, zt, normed, gate, maskv, wproj, wg, wo, gains,
    asend, arecv, bsend, brecv, rpair, lpair, cbuf, crecv, dsend, drecv,
    stage, send_sem, recv_sem,
):
    r = lax.axis_index("row")
    c = lax.axis_index("col")
    core = r % 2
    rb = r // 2
    z = c % 8
    xl = c // 8

    def col_peer(n):
        hop = n // 2
        away = (hop + 1) // 2 * (1 - 2 * (hop % 2))
        return (xl + n % 2) % 2 * 8 + (z + away + 8) % 8

    def row_peer(n):
        return (rb // 2 + n // 2) % 4 * 2 + (rb + n) % 2

    barrier = pltpu.get_barrier_semaphore()

    def greet(row, col):
        pl.semaphore_signal(barrier, inc=1, device_id=(row, col), device_id_type=MESH)

    loop(16, lambda n: greet(r, col_peer(n)), 1)
    loop(8, lambda n: greet(row_peer(n) * 2 + core, c), 1)
    greet(rb * 2 + 1 - core, c)

    def remote(src, dst, u, phase, q, row, col):
        return pltpu.make_async_remote_copy(
            src_ref=src, dst_ref=dst,
            send_sem=send_sem.at[u, phase, q], recv_sem=recv_sem.at[u, phase, q],
            device_id=(row, col), device_id_type=MESH,
        )

    for u in range(2):
        wt = [win_ref[u, t].astype(F32).T for t in range(4)]
        for half in range(2):
            lo, hi = wt[half], wt[half + 2]
            both = jnp.concatenate([lo.reshape(16, 1, 8, 128), hi.reshape(16, 1, 8, 128)], axis=1)
            wproj[u, half] = both.reshape(256, 128).astype(BF16)
        wg[u] = wgate_ref[u].astype(F32).T.astype(BF16)
        wo[u] = wout_ref[u].astype(F32).T.astype(BF16)
        gains[u, 0] = jnp.broadcast_to(gin_ref[u : u + 1, :], (128, 128)).T
        gains[u, 1] = jnp.broadcast_to(gout_ref[u : u + 1, :], (128, 128)).T

    mask_row = jnp.broadcast_to(mask_ref[...].astype(F32), (8, 768)).astype(BF16)
    place = lax.broadcasted_iota(jnp.int32, (768, 128), 0)
    lane = lax.broadcasted_iota(jnp.int32, (768, 128), 1)
    col_masks = [
        nn(mask_row, (place == c * 48 + kh * 16 + (lane & 15)).astype(F32).astype(BF16)) for kh in range(3)
    ]

    def fill_masks(ihg):
        rows = nn(mask_row, (place == r * 48 + ihg * 8 + (lane >> 4)).astype(F32).astype(BF16))
        for kh in range(3):
            maskv[ihg // 2 * 3 + kh, ihg % 2] = rows * col_masks[kh]

    loop(6, fill_masks)

    def load_tile(ihg):
        for kh in range(3):
            block = x_ref[pl.ds(ihg * 8, 8), kh * 16 : kh * 16 + 16, :].reshape(128, 128)
            zt[ihg // 2 * 3 + kh, ihg % 2] = block.astype(F32).T

    loop(6, load_tile)

    def load_zt(i):
        return jnp.concatenate([zt[i, 0], zt[i, 1]], axis=1)

    def wide(block):
        return jnp.concatenate([block, block], axis=1)

    def project(u, q, kh, values):
        i = q * 3 + kh
        nrm = norm_rows(values, wide(gains[u, 0]))
        normed[i] = nrm
        mask = jnp.concatenate([maskv[i, 0], maskv[i, 1]], axis=1)[0:1]
        for h in range(4):
            val = nn(wproj[u, 0, h * 64 : h * 64 + 64], nrm)
            gat = nn(wproj[u, 1, h * 64 : h * 64 + 64], nrm)
            y = (val * sigmoid(gat) * mask).astype(BF16)
            for ih in range(2):
                asend[u, h * 4 : h * 4 + 4, q, kh, ih] = y[:, ih * 128 : ih * 128 + 128].reshape(4, 16, 128)

    def send_cols(u, q):
        def one(n):
            s = col_peer(n)
            remote(asend.at[u, s, q], arecv.at[u, c, q], u, COLS_OUT, q, r, s).start()

        loop(16, one, 1)
        arecv[u, c, q] = asend[u, c, q]

    def gates(u):
        def one(i):
            gate[i] = sigmoid(nn(wg[u], normed[i]))

        loop(9, one)

    def fill_perm():
        row = lax.broadcasted_iota(jnp.int32, (128, 128), 0)
        col = lax.broadcasted_iota(jnp.int32, (128, 128), 1)
        same = (row & 15) == (col & 15)

        def one(n):
            p = n // 8
            g = n % 8
            hit = same & ((row >> 4) == g) & ((col >> 4) == p)
            perm[g, pl.ds(pl.multiple_of(p * 128, 128), 128), :] = hit.astype(F32).astype(BF16)

        loop(64, one)

    def regroup_out(u, q):
        wait_bytes(arecv.at[u, pl.ds(0, 15), q], recv_sem.at[u, COLS_OUT, q])
        x = jnp.concatenate([arecv[u, 2 * p : 2 * p + 2, q].reshape(192, 128) for p in range(8)], axis=1)

        def one(t):
            y = nn(x, jnp.concatenate([perm[2 * t], perm[2 * t + 1]], axis=1))
            for hh in range(2):
                part = y[:, hh * 128 : hh * 128 + 128].reshape(2, 3, 2, 2, 8, 128)
                for ch in range(2):
                    for kh in range(3):
                        for ih in range(2):
                            for lr in range(2):
                                stage[lr, ch * 3 + kh, pl.ds(ih * 8 + 2 * t + hh, 8, stride=16), :] = part[ch, kh, ih, lr]

        loop(4, one)

        def pack(d):
            bsend[u, q, d] = stage[:, :, pl.ds(pl.multiple_of(d * 16, 16), 16), :].astype(BF16)

        loop(8, pack)

        def one_send(n):
            peer = row_peer(n)
            remote(bsend.at[u, q, peer], brecv.at[u, q, rb], u, ROWS_OUT, q, peer * 2 + core, c).start()

        loop(8, one_send, 1)
        brecv[u, q, rb] = bsend[u, q, rb]

    def pair_copies(u, q):
        other = rb * 2 + 1 - core
        copies = [remote(brecv.at[u, q, :, 1], rpair.at[u, q], u, PAIR_RIGHT, q, other, c)]
        if u == 1:
            copies.append(
                remote(brecv.at[u, q, :, 0, pl.ds((1 - core) * 3, 3)], lpair.at[q], u, PAIR_LEFT, q, other, c)
            )
        return copies

    def exchange(u, q):
        wait_bytes(brecv.at[u, q, pl.ds(0, 7)], recv_sem.at[u, ROWS_OUT, q])
        for copy in pair_copies(u, q):
            copy.start()

    def product_out(qi):
        u = 0
        left = jnp.concatenate([brecv[u, qi, :, 0, m].reshape(128, 128) for m in range(6)], axis=1)
        for jh in range(3):
            for own in range(2):
                if own:
                    right = jnp.concatenate([brecv[u, jh, :, 1, m].reshape(128, 128) for m in range(6)], axis=1)
                    m_out = core * 3 + jh
                else:
                    right = jnp.concatenate([rpair[u, jh, :, m].reshape(128, 128) for m in range(6)], axis=1)
                    m_out = (1 - core) * 3 + jh
                cbuf[u, qi, :, m_out] = nt(left, right).astype(BF16).reshape(8, 16, 128)

    def product_in(qi):
        u = 1
        mine = brecv[u, :, :, 0, core * 3 + qi].reshape(384, 128).astype(F32).T.astype(BF16)
        theirs = lpair[:, :, qi].reshape(384, 128).astype(F32).T.astype(BF16)
        for m in range(0, 6, 2):
            right = jnp.concatenate([brecv[u, :, :, 1, m + k].reshape(384, 128) for k in range(2)], axis=1)
            extra = jnp.concatenate([rpair[u, :, :, m + k].reshape(384, 128) for k in range(2)], axis=1)
            both = (nn(mine, right) + nn(theirs, extra)).astype(BF16)
            for k in range(2):
                cbuf[u, qi, :, m + k] = both[:, k * 128 : k * 128 + 128].reshape(8, 16, 128)

    def send_products(u, qi):
        def one(n):
            peer = row_peer(n)
            remote(cbuf.at[u, qi, peer], crecv.at[u, qi, rb], u, ROWS_BACK, qi, peer * 2 + core, c).start()

        loop(8, one, 1)
        crecv[u, qi, rb] = cbuf[u, qi, rb]

    def regroup_back(u, q):
        wait_bytes(crecv.at[u, q, pl.ds(0, 7)], recv_sem.at[u, ROWS_BACK, q])

        def unpack(d):
            stage[0, :, pl.ds(pl.multiple_of(d * 16, 16), 16), :] = crecv[u, q, d].astype(F32)

        loop(8, unpack)
        columns = []
        for il in range(8):
            rows = [stage[0, m, pl.ds(ih * 8 + il, 8, stride=16), :] for m in range(6) for ih in range(2)]
            columns.append(jnp.concatenate(rows, axis=0).astype(BF16))
        x = jnp.concatenate(columns, axis=1)

        def one(t):
            y = nn(x, jnp.concatenate([perm[2 * t], perm[2 * t + 1]], axis=1)).astype(BF16)
            for hh in range(2):
                part = y[:, hh * 128 : hh * 128 + 128].reshape(2, 3, 16, 128)
                dsend[u, pl.ds(2 * (2 * t + hh), 2), q] = part

        loop(4, one)

        def one_send(n):
            s = col_peer(n)
            remote(dsend.at[u, s, q], drecv.at[u, c, q], u, COLS_BACK, q, r, s).start()

        loop(16, one_send, 1)
        drecv[u, c, q] = dsend[u, c, q]

    def finish_chunk(u, q):
        wait_bytes(drecv.at[u, pl.ds(0, 15), q], recv_sem.at[u, COLS_BACK, q])

        def one(kh):
            i = q * 3 + kh
            got = drecv[u, :, q, kh].astype(F32).reshape(16, 2, 8, 128)
            mixed = jnp.concatenate([got[:, 0].reshape(128, 128), got[:, 1].reshape(128, 128)], axis=1)
            branch = nn(wo[u], norm_rows(mixed, wide(gains[u, 1])))
            new = (load_zt(i) + gate[i] * branch).astype(BF16).astype(F32)
            if u == 0:
                for ih in range(2):
                    zt[i, ih] = new[:, ih * 128 : ih * 128 + 128]
                project(1, q, kh, new)
            else:
                for ih in range(2):
                    tile = new[:, ih * 128 : ih * 128 + 128].T.astype(BF16).reshape(8, 16, 128)
                    out_ref[pl.ds((q * 2 + ih) * 8, 8), pl.ds(pl.multiple_of(kh * 16, 16), 16), :] = tile

        loop(3, one)

    def first(q):
        loop(3, lambda kh: project(0, q, kh, load_zt(q * 3 + kh)))

    first(0)
    pl.semaphore_wait(barrier, 23)
    send_cols(0, 0)
    for q in (1, 2):
        first(q)
        send_cols(0, q)
    fill_perm()
    for u in range(2):
        gates(u)
        regroup_out(u, 0)

        def middle(q):
            regroup_out(u, q)
            exchange(u, q - 1)

        loop(3, middle, 1)
        exchange(u, 2)
        for q in range(3):
            for copy in pair_copies(u, q):
                copy.wait_recv()

        def products(qi):
            (product_out if u == 0 else product_in)(qi)
            send_products(u, qi)

        loop(3, products)
        loop(3, lambda q: regroup_back(u, q))

        def close(q):
            finish_chunk(u, q)
            if u == 0:
                send_cols(1, q)

        loop(3, close)

    for u in range(2):

        def drain(q):
            wait_bytes(asend.at[u, pl.ds(0, 15), q], send_sem.at[u, COLS_OUT, q])
            wait_bytes(bsend.at[u, q, pl.ds(0, 7)], send_sem.at[u, ROWS_OUT, q])
            for copy in pair_copies(u, q):
                copy.wait_send()
            wait_bytes(cbuf.at[u, q, pl.ds(0, 7)], send_sem.at[u, ROWS_BACK, q])
            wait_bytes(dsend.at[u, pl.ds(0, 15), q], send_sem.at[u, COLS_BACK, q])

        loop(3, drain)


def body(pair_state, residue_mask, weight_in, weight_gate, weight_out, gain_in, gain_out):
    vmem = pl.BlockSpec(memory_space=pltpu.VMEM)
    weights = weight_in.transpose(0, 2, 1, 3)
    mask = residue_mask.reshape(1, 768)
    return pl.pallas_call(
        kernel,
        out_shape=jax.ShapeDtypeStruct((48, 48, 128), BF16),
        in_specs=[vmem] * 7,
        out_specs=vmem,
        scratch_shapes=[
            pltpu.VMEM((8, 1024, 128), BF16),
            pltpu.VMEM((9, 2, 128, 128), F32),
            pltpu.VMEM((9, 128, 256), BF16),
            pltpu.VMEM((9, 128, 256), F32),
            pltpu.VMEM((9, 2, 8, 128), F32),
            pltpu.VMEM((2, 2, 256, 128), BF16),
            pltpu.VMEM((2, 128, 128), BF16),
            pltpu.VMEM((2, 128, 128), BF16),
            pltpu.VMEM((2, 2, 128, 128), F32),
            pltpu.VMEM((2, 16, 3, 3, 2, 16, 128), BF16),
            pltpu.VMEM((2, 16, 3, 3, 2, 16, 128), BF16),
            pltpu.VMEM((2, 3, 8, 2, 6, 16, 128), BF16),
            pltpu.VMEM((2, 3, 8, 2, 6, 16, 128), BF16),
            pltpu.VMEM((2, 3, 8, 6, 16, 128), BF16),
            pltpu.VMEM((3, 8, 3, 16, 128), BF16),
            pltpu.VMEM((2, 3, 8, 6, 16, 128), BF16),
            pltpu.VMEM((2, 3, 8, 6, 16, 128), BF16),
            pltpu.VMEM((2, 16, 3, 3, 16, 128), BF16),
            pltpu.VMEM((2, 16, 3, 3, 16, 128), BF16),
            pltpu.VMEM((2, 6, 128, 128), F32),
            pltpu.SemaphoreType.DMA((2, 6, 3)),
            pltpu.SemaphoreType.DMA((2, 6, 3)),
        ],
        compiler_params=pltpu.CompilerParams(
            collective_id=0, has_side_effects=True, vmem_limit_bytes=48 * 1024 * 1024
        ),
        name="triangle",
    )(pair_state, mask, weights, weight_gate, weight_out, gain_in, gain_out)


def solution(mesh):
    return jax.shard_map(
        body,
        mesh=mesh,
        in_specs=(P("row", "col", None), P(), P(), P(), P(), P(), P()),
        out_specs=P("row", "col", None),
        check_vma=False,
    )
```

profile of v0, /device:TPU:1, one launch (start us, length us, event | category | flops | bytes accessed | tf_op | source)
XLA Modules:
  0.0 136.0 jit_solution(16726975085931595611)
XLA Ops:
  0.0 0.7 reshape.3.mask_ref
  0.7 0.0 copy-start.1
  0.7 0.0 copy-start.2
  0.7 0.0 copy-start.4
  0.7 1.0 copy.10
  1.7 0.0 copy-start.3
  1.7 0.0 copy-done.1
  1.7 0.0 copy-done.2
  1.8 0.0 copy-done.4
  1.8 0.6 copy-done.3
  2.4 0.0 copy-start
  2.4 1.1 copy-done
  3.5 131.7 %triangle.1 = bf16[48,48,128]{2,1,0:T(8,128)(2,1)S(1)} custom-call(bf16[48,48,128]{2,1,0:T(8,128)(2,1)S(1)} %copy-done, s32[1,768]{1,0:T(1,128)S(1)} %reshape.3.mask_ref, bf16[2,4,128,128]{3,2,1,0:T(8,128)(2,1)S(1)} %bitcast.3, bf16[2,128,128]{2,1,0:T(8,128)(2,1)S(1)} %copy-done.1, bf16[2,128,128]{2,1,0:T(8,128)(2,1)S(1)} %copy-done.2, ...), custom_call_target="tpu_custom_call" | custom-call | tf_op jit(solution)/shard_map/triangle/pallas_call | solution.py:341
  135.1 0.8 copy.12
Async XLA Ops:
  0.7 1.0 copy-start.1
  0.7 1.1 copy-start.2
  0.7 1.1 copy-start.4
  1.7 0.7 copy-start.3
  2.4 1.1 copy-start
where the time goes:
time: 136 us
  Pallas kernels  132 us (97%)
  local copies, waits for them, and re-layouts  4.25 us (3%)
    pallas_call x1, Pallas kernels, body(): pl.pallas_call(kernel, out_shape=jax.ShapeDtypeStruct((48, 48, 128), BF16...  132 us
    unnamed x12, local copies, waits for them, and re-layouts  3.56 us

commit v1 on v0

v1 whole, which is shorter than its diff:
```python
import jax
import jax.numpy as jnp
from jax import lax
from jax.experimental import pallas as pl
from jax.experimental.pallas import tpu as pltpu
from jax.sharding import PartitionSpec as P

MESH = pl.DeviceIdType.MESH
F32 = jnp.float32
BF16 = jnp.bfloat16
EPS = 1e-5
COLS_OUT, ROWS_OUT, PAIR, ROWS_BACK, COLS_BACK = range(5)
BLOCKS = ((0, 0), (0, 1), (1, 0), (1, 1), (0, 2), (1, 2), (2, 0), (2, 1), (2, 2))
WAVES = ((0, 1), (1, 4), (4, 6), (6, 7), (7, 9))


def sigmoid(x):
    return 0.5 * jnp.tanh(0.5 * x) + 0.5


def norm_rows(values, gain):
    mean = jnp.sum(values, axis=0, keepdims=True) * (1.0 / 128.0)
    centered = values - mean
    var = jnp.sum(centered * centered, axis=0, keepdims=True) * (1.0 / 128.0)
    return (centered * lax.rsqrt(var + EPS) * gain).astype(BF16)


def nn(a, b):
    return lax.dot_general(a, b, (((1,), (0,)), ((), ())), preferred_element_type=F32)


def nt(a, b):
    return lax.dot_general(a, b, (((1,), (1,)), ((), ())), preferred_element_type=F32)


def tn(a, b):
    return lax.dot_general(a, b, (((0,), (0,)), ((), ())), preferred_element_type=F32)


def loop(n, body, start=0):
    def step(i, carry):
        body(i)
        return carry

    lax.fori_loop(start, n, step, 0)


def wait_bytes(ref, sem):
    pltpu.make_async_copy(ref, ref, sem).wait()


def kernel(
    x_ref, mask_ref, win_ref, wgate_ref, wout_ref, gin_ref, gout_ref, out_ref,
    perm, zt, normed, gate, maskv, wproj, wg, wo, gains,
    asend, arecv, bsend, brecv, rpair, lpair, lturn, cbuf, crecv, dsend, drecv,
    stage, stage_back, send_sem, recv_sem,
):
    r = lax.axis_index("row")
    c = lax.axis_index("col")
    core = r % 2
    rb = r // 2
    z = c % 8
    xl = c // 8

    def col_peer(n):
        hop = n // 2
        away = (hop + 1) // 2 * (1 - 2 * (hop % 2))
        return (xl + n % 2) % 2 * 8 + (z + away + 8) % 8

    def row_peer(n):
        return (rb // 2 + n // 2) % 4 * 2 + (rb + n) % 2

    barrier = pltpu.get_barrier_semaphore()

    def greet(row, col):
        pl.semaphore_signal(barrier, inc=1, device_id=(row, col), device_id_type=MESH)

    loop(16, lambda n: greet(r, col_peer(n)), 1)
    loop(8, lambda n: greet(row_peer(n) * 2 + core, c), 1)
    greet(rb * 2 + 1 - core, c)

    def remote(src, dst, u, phase, q, row, col):
        return pltpu.make_async_remote_copy(
            src_ref=src, dst_ref=dst,
            send_sem=send_sem.at[u, phase, q], recv_sem=recv_sem.at[u, phase, q],
            device_id=(row, col), device_id_type=MESH,
        )

    for u in range(2):
        for t in range(4):
            wproj[u, t] = win_ref[u, t].astype(F32).T.astype(BF16)
        wg[u] = wgate_ref[u].astype(F32).T.astype(BF16)
        wo[u] = wout_ref[u].astype(F32).T.astype(BF16)
        gains[u, 0] = jnp.broadcast_to(gin_ref[u : u + 1, :], (128, 128)).T
        gains[u, 1] = jnp.broadcast_to(gout_ref[u : u + 1, :], (128, 128)).T

    mask_row = jnp.broadcast_to(mask_ref[...].astype(F32), (8, 768)).astype(BF16)
    place = lax.broadcasted_iota(jnp.int32, (768, 128), 0)
    lane = lax.broadcasted_iota(jnp.int32, (768, 128), 1)
    col_masks = [
        nn(mask_row, (place == c * 48 + kh * 16 + (lane & 15)).astype(F32).astype(BF16)) for kh in range(3)
    ]

    def fill_masks(ihg):
        rows = nn(mask_row, (place == r * 48 + ihg * 8 + (lane >> 4)).astype(F32).astype(BF16))
        for kh in range(3):
            maskv[ihg // 2 * 3 + kh, ihg % 2] = rows * col_masks[kh]

    loop(6, fill_masks)

    def load_tile(ihg):
        for kh in range(3):
            block = x_ref[pl.ds(ihg * 8, 8), kh * 16 : kh * 16 + 16, :].reshape(128, 128)
            zt[ihg // 2 * 3 + kh, ihg % 2] = block.astype(F32).T

    loop(6, load_tile)

    def load_zt(i):
        return jnp.concatenate([zt[i, 0], zt[i, 1]], axis=1)

    def wide(block):
        return jnp.concatenate([block, block], axis=1)

    def project(u, q, kh, values):
        i = q * 3 + kh
        nrm = norm_rows(values, wide(gains[u, 0]))
        normed[i] = nrm
        mask = jnp.concatenate([maskv[i, 0], maskv[i, 1]], axis=1)[0:1]
        chunk, inner = (q, kh) if u == 0 else (kh, q)
        for side in (1, 0):
            for h in range(2):
                val = nn(wproj[u, 2 * side, h * 64 : h * 64 + 64], nrm)
                gat = nn(wproj[u, 2 * side + 1, h * 64 : h * 64 + 64], nrm)
                y = (val * sigmoid(gat) * mask).reshape(8, 8, 256)
                y = jnp.concatenate([y[:, :, :128], y[:, :, 128:]], axis=1).astype(BF16)
                asend[u, side, chunk, h * 8 : h * 8 + 8, inner] = y

    def send_cols(u, chunk):
        for side in (1, 0):
            h = 2 * chunk + 1 - side

            def one(n):
                s = col_peer(n)
                remote(asend.at[u, side, chunk, s], arecv.at[u, side, chunk, c], u, COLS_OUT, h, r, s).start()

            loop(16, one, 1)
            arecv[u, side, chunk, c] = asend[u, side, chunk, c]

    def gates(u):
        def one(i):
            gate[i] = sigmoid(nn(wg[u], normed[i]))

        loop(9, one)

    def fill_perm():
        row = lax.broadcasted_iota(jnp.int32, (128, 128), 0)
        col = lax.broadcasted_iota(jnp.int32, (128, 128), 1)
        same = (row & 15) == (col & 15)

        def one(n):
            p = n // 8
            g = n % 8
            hit = same & ((row >> 4) == g) & ((col >> 4) == p)
            perm[g, pl.ds(pl.multiple_of(p * 128, 128), 128), :] = hit.astype(F32).astype(BF16)

        loop(64, one)

    def regroup_out(u, h):
        side, chunk = 1 - h % 2, h // 2
        wait_bytes(arecv.at[u, side, chunk, pl.ds(0, 15)], recv_sem.at[u, COLS_OUT, h])
        x = jnp.concatenate(
            [arecv[u, side, chunk, 2 * p : 2 * p + 2].reshape(96, 128) for p in range(8)], axis=1
        )

        def one(t):
            y = nn(x, jnp.concatenate([perm[2 * t], perm[2 * t + 1]], axis=1))
            for hh in range(2):
                part = y[:, hh * 128 : hh * 128 + 128].reshape(6, 2, 8, 128)
                for m in range(6):
                    for ih in range(2):
                        stage[m, pl.ds(ih * 8 + 2 * t + hh, 8, stride=16), :] = part[m, ih]

        loop(4, one)

        def pack(d):
            bsend[u, side, chunk, d] = stage[:, pl.ds(pl.multiple_of(d * 16, 16), 16), :].astype(BF16)

        loop(8, pack)

        def one_send(n):
            peer = row_peer(n)
            remote(
                bsend.at[u, side, chunk, peer], brecv.at[u, side, chunk, rb], u, ROWS_OUT, h, peer * 2 + core, c
            ).start()

        loop(8, one_send, 1)
        brecv[u, side, chunk, rb] = bsend[u, side, chunk, rb]

    def pair_copy(u, h):
        side, chunk = 1 - h % 2, h // 2
        other = rb * 2 + 1 - core
        if side == 1:
            return remote(brecv.at[u, 1, chunk], rpair.at[u, chunk], u, PAIR, h, other, c)
        return remote(
            brecv.at[u, 0, chunk, :, pl.ds((1 - core) * 3, 3)], lpair.at[chunk], u, PAIR, h, other, c
        )

    def exchange(u, h):
        side, chunk = 1 - h % 2, h // 2
        wait_bytes(brecv.at[u, side, chunk, pl.ds(0, 7)], recv_sem.at[u, ROWS_OUT, h])
        if side == 1 or u == 1:
            pair_copy(u, h).start()

    def exchanged(u, h):
        if h % 2 == 0 or u == 1:
            pair_copy(u, h).wait_recv()
        if h % 2 == 1 and u == 1:
            chunk = h // 2
            mine = brecv[u, 0, chunk, :, pl.ds(core * 3, 3)].reshape(384, 128)
            theirs = lpair[chunk].reshape(384, 128)
            lturn[chunk, 0] = mine.astype(F32).T.astype(BF16)
            lturn[chunk, 1] = theirs.astype(F32).T.astype(BF16)

    def product(u, n):
        qi, jh = BLOCKS[n]
        if u == 0:
            left = jnp.concatenate([brecv[u, 0, qi, :, m].reshape(128, 128) for m in range(6)], axis=1)
            mine = jnp.concatenate([brecv[u, 1, jh, :, m].reshape(128, 128) for m in range(6)], axis=1)
            theirs = jnp.concatenate([rpair[u, jh, :, m].reshape(128, 128) for m in range(6)], axis=1)
            both = nt(left, jnp.concatenate([mine, theirs], axis=0)).astype(BF16)
            places = (core, 1 - core)
        else:
            mine = jnp.concatenate(
                [brecv[u, 1, jh, :, 3 * k : 3 * k + 3].reshape(384, 128) for k in range(2)], axis=1
            )
            theirs = jnp.concatenate(
                [rpair[u, jh, :, 3 * k : 3 * k + 3].reshape(384, 128) for k in range(2)], axis=1
            )
            both = (nn(lturn[qi, 0], mine) + nn(lturn[qi, 1], theirs)).astype(BF16)
            places = (0, 1)
        for k in range(2):
            cbuf[u, :, n, places[k]] = both[:, k * 128 : k * 128 + 128].reshape(8, 16, 128)

    def products(u, w):
        begin, end = WAVES[w]
        for n in range(begin, end):
            product(u, n)
        span = pl.ds(begin, end - begin)

        def one(n):
            peer = row_peer(n)
            remote(
                cbuf.at[u, peer, span], crecv.at[u, rb, span], u, ROWS_BACK, w, peer * 2 + core, c
            ).start()

        loop(8, one, 1)
        crecv[u, rb, span] = cbuf[u, rb, span]

    def regroup_back(u, w):
        begin, end = WAVES[w]
        size = end - begin
        span = pl.ds(begin, size)
        wait_bytes(crecv.at[u, pl.ds(0, 7), span], recv_sem.at[u, ROWS_BACK, w])

        def unpack(d):
            stage_back[0:size, :, pl.ds(pl.multiple_of(d * 16, 16), 16), :] = crecv[u, d, span].astype(F32)

        loop(8, unpack)
        columns = []
        for il in range(8):
            rows = [
                stage_back[n, ch, pl.ds(ih * 8 + il, 8, stride=16), :]
                for n in range(size) for ch in range(2) for ih in range(2)
            ]
            columns.append(jnp.concatenate(rows, axis=0).astype(BF16))
        x = jnp.concatenate(columns, axis=1)

        def one(t):
            y = nn(x, jnp.concatenate([perm[2 * t], perm[2 * t + 1]], axis=1)).astype(BF16)
            for hh in range(2):
                part = y[:, hh * 128 : hh * 128 + 128].reshape(size, 2, 16, 128)
                for ch in range(2):
                    dsend[u, 2 * (2 * t + hh) + ch, span] = part[:, ch]

        loop(4, one)

        def one_send(n):
            s = col_peer(n)
            remote(dsend.at[u, s, span], drecv.at[u, c, span], u, COLS_BACK, w, r, s).start()

        loop(16, one_send, 1)
        drecv[u, c, span] = dsend[u, c, span]

    def arrive_back(u, w):
        begin, end = WAVES[w]
        wait_bytes(drecv.at[u, pl.ds(0, 15), pl.ds(begin, end - begin)], recv_sem.at[u, COLS_BACK, w])

    def finish(u, n):
        q, kh = BLOCKS[n]
        i = q * 3 + kh
        got = drecv[u, :, n].astype(F32).reshape(16, 2, 8, 128)
        mixed = jnp.concatenate([got[:, 0].reshape(128, 128), got[:, 1].reshape(128, 128)], axis=1)
        branch = nn(wo[u], norm_rows(mixed, wide(gains[u, 1])))
        new = (load_zt(i) + gate[i] * branch).astype(BF16).astype(F32)
        for ih in range(2):
            half = new[:, ih * 128 : ih * 128 + 128]
            if u == 0:
                zt[i, ih] = half
            else:
                rows = (q * 2 + ih) * 8
                out_ref[rows : rows + 8, kh * 16 : kh * 16 + 16, :] = half.T.astype(BF16).reshape(8, 16, 128)
        if u == 0:
            project(1, q, kh, new)

    def first(q):
        loop(3, lambda kh: project(0, q, kh, load_zt(q * 3 + kh)))

    first(0)
    pl.semaphore_wait(barrier, 23)
    send_cols(0, 0)
    for q in (1, 2):
        first(q)
        send_cols(0, q)
    fill_perm()
    for u in range(2):
        gates(u)
        regroup_out(u, 0)
        regroup_out(u, 1)
        exchange(u, 0)
        regroup_out(u, 2)
        exchange(u, 1)
        exchanged(u, 0)
        exchanged(u, 1)
        products(u, 0)
        regroup_out(u, 3)
        exchange(u, 2)
        regroup_out(u, 4)
        exchange(u, 3)
        exchanged(u, 2)
        exchanged(u, 3)
        products(u, 1)
        regroup_back(u, 0)
        regroup_out(u, 5)
        exchange(u, 4)
        regroup_back(u, 1)
        exchanged(u, 4)
        products(u, 2)
        exchange(u, 5)
        exchanged(u, 5)
        products(u, 3)
        products(u, 4)
        regroup_back(u, 2)
        arrive_back(u, 0)
        finish(u, 0)
        arrive_back(u, 1)
        for n in (1, 2, 3):
            finish(u, n)
        regroup_back(u, 3)
        regroup_back(u, 4)
        arrive_back(u, 2)
        for n in (4, 5):
            finish(u, n)
        arrive_back(u, 3)
        finish(u, 6)
        if u == 0:
            send_cols(1, 0)
        arrive_back(u, 4)
        for n in (7, 8):
            finish(u, n)
            if u == 0:
                send_cols(1, n - 6)

    for u in range(2):
        for h in range(6):
            side, chunk = 1 - h % 2, h // 2
            wait_bytes(asend.at[u, side, chunk, pl.ds(0, 15)], send_sem.at[u, COLS_OUT, h])
            wait_bytes(bsend.at[u, side, chunk, pl.ds(0, 7)], send_sem.at[u, ROWS_OUT, h])
            if side == 1 or u == 1:
                pair_copy(u, h).wait_send()
        for w, (begin, end) in enumerate(WAVES):
            span = pl.ds(begin, end - begin)
            wait_bytes(cbuf.at[u, pl.ds(0, 7), span], send_sem.at[u, ROWS_BACK, w])
            wait_bytes(dsend.at[u, pl.ds(0, 15), span], send_sem.at[u, COLS_BACK, w])


def body(pair_state, residue_mask, weight_in, weight_gate, weight_out, gain_in, gain_out):
    vmem = pl.BlockSpec(memory_space=pltpu.VMEM)
    weights = weight_in.transpose(0, 2, 1, 3)
    mask = residue_mask.reshape(1, 768)
    return pl.pallas_call(
        kernel,
        out_shape=jax.ShapeDtypeStruct((48, 48, 128), BF16),
        in_specs=[vmem] * 7,
        out_specs=vmem,
        scratch_shapes=[
            pltpu.VMEM((8, 1024, 128), BF16),
            pltpu.VMEM((9, 2, 128, 128), F32),
            pltpu.VMEM((9, 128, 256), BF16),
            pltpu.VMEM((9, 128, 256), F32),
            pltpu.VMEM((9, 2, 8, 128), F32),
            pltpu.VMEM((2, 4, 128, 128), BF16),
            pltpu.VMEM((2, 128, 128), BF16),
            pltpu.VMEM((2, 128, 128), BF16),
            pltpu.VMEM((2, 2, 128, 128), F32),
            pltpu.VMEM((2, 2, 3, 16, 3, 16, 128), BF16),
            pltpu.VMEM((2, 2, 3, 16, 3, 16, 128), BF16),
            pltpu.VMEM((2, 2, 3, 8, 6, 16, 128), BF16),
            pltpu.VMEM((2, 2, 3, 8, 6, 16, 128), BF16),
            pltpu.VMEM((2, 3, 8, 6, 16, 128), BF16),
            pltpu.VMEM((3, 8, 3, 16, 128), BF16),
            pltpu.VMEM((3, 2, 128, 384), BF16),
            pltpu.VMEM((2, 8, 9, 2, 16, 128), BF16),
            pltpu.VMEM((2, 8, 9, 2, 16, 128), BF16),
            pltpu.VMEM((2, 16, 9, 16, 128), BF16),
            pltpu.VMEM((2, 16, 9, 16, 128), BF16),
            pltpu.VMEM((6, 128, 128), F32),
            pltpu.VMEM((3, 2, 128, 128), F32),
            pltpu.SemaphoreType.DMA((2, 5, 6)),
            pltpu.SemaphoreType.DMA((2, 5, 6)),
        ],
        compiler_params=pltpu.CompilerParams(
            collective_id=0, has_side_effects=True, vmem_limit_bytes=48 * 1024 * 1024
        ),
        name="triangle",
    )(pair_state, mask, weights, weight_gate, weight_out, gain_in, gain_out)


def solution(mesh):
    return jax.shard_map(
        body,
        mesh=mesh,
        in_specs=(P("row", "col", None), P(), P(), P(), P(), P(), P()),
        out_specs=P("row", "col", None),
        check_vma=False,
    )
```

time: 136 us -> 126 us (0.926)
  Pallas kernels: 132 us -> 122 us
    pallas_call x1, Pallas kernels: 132 us -> 122 us  [body(): pl.pallas_call(kernel, out_shape=jax.ShapeDtypeStruct((48, 48, 128), BF16...]
where the time goes in v1:
time: 126 us
  Pallas kernels  122 us (97%)
  local copies, waits for them, and re-layouts  4.25 us (3%)
    pallas_call x1, Pallas kernels, body(): pl.pallas_call(kernel, out_shape=jax.ShapeDtypeStruct((48, 48, 128), BF16...  122 us
    unnamed x12, local copies, waits for them, and re-layouts  3.56 us

profile of v1, /device:TPU:1, one launch (start us, length us, event | category | flops | bytes accessed | tf_op | source)
XLA Modules:
  0.0 125.9 jit_solution(1547150794169024380)
XLA Ops:
  0.0 0.7 reshape.3.mask_ref
  0.7 0.0 copy-start.1
  0.7 0.0 copy-start.2
  0.7 0.0 copy-start.4
  0.7 1.0 copy.10
  1.7 0.0 copy-start.3
  1.7 0.0 copy-done.1
  1.7 0.0 copy-done.2
  1.8 0.0 copy-done.4
  1.8 0.6 copy-done.3
  2.4 0.0 copy-start
  2.4 1.1 copy-done
  3.5 121.6 %triangle.1 = bf16[48,48,128]{2,1,0:T(8,128)(2,1)S(1)} custom-call(bf16[48,48,128]{2,1,0:T(8,128)(2,1)S(1)} %copy-done, s32[1,768]{1,0:T(1,128)S(1)} %reshape.3.mask_ref, bf16[2,4,128,128]{3,2,1,0:T(8,128)(2,1)S(1)} %bitcast.3, bf16[2,128,128]{2,1,0:T(8,128)(2,1)S(1)} %copy-done.1, bf16[2,128,128]{2,1,0:T(8,128)(2,1)S(1)} %copy-done.2, ...), custom_call_target="tpu_custom_call" | custom-call | tf_op jit(solution)/shard_map/triangle/pallas_call | solution.py:390
  125.1 0.8 copy.12
Async XLA Ops:
  0.7 1.0 copy-start.1
  0.7 1.1 copy-start.2
  0.7 1.1 copy-start.4
  1.7 0.7 copy-start.3
  2.4 1.1 copy-start

commit v2 on v1

v2 whole, which is shorter than its diff:
```python
import jax
import jax.numpy as jnp
from jax import lax
from jax.experimental import pallas as pl
from jax.experimental.pallas import tpu as pltpu
from jax.sharding import PartitionSpec as P

MESH = pl.DeviceIdType.MESH
F32 = jnp.float32
BF16 = jnp.bfloat16
EPS = 1e-5
COLS_OUT, ROWS_OUT, PAIR, ROWS_BACK, COLS_BACK, RIGHT_ROWS, RIGHT_COLS = range(7)
AHEAD = 2
BLOCKS = ((0, 0), (1, 0), (2, 0), (0, 1), (1, 1), (2, 1), (0, 2), (1, 2), (2, 2))
WAVES = ((0, 2), (2, 3), (3, 6), (6, 9))
PLAN = (
    ("out", 0), ("left", 2), ("mid", 0), ("out", 1), ("mid", 1), ("out", 2), ("take", 0), ("take", 1), ("in", 0), ("mid", 2), ("gates", 0), ("turn", 0), ("turn", 1), ("take", 2), ("pair", 0), ("product", 0), ("turn", 2), ("product", 1), ("in", 1), ("back", 0), ("back", 1), ("pair", 1), ("product", 2), ("in", 2), ("land", 0), ("finish", 0), ("finish", 1), ("pair", 2), ("product", 3), ("back", 2), ("land", 1), ("finish", 2), ("next", 0), ("back", 3), ("land", 2), ("finish", 3), ("finish", 4), ("finish", 5), ("next", 1), ("land", 3), ("finish", 6), ("finish", 7), ("finish", 8), ("next", 2),
)


def sigmoid(x):
    return 0.5 * jnp.tanh(0.5 * x) + 0.5


def norm_rows(values, gain):
    mean = jnp.sum(values, axis=0, keepdims=True) * (1.0 / 128.0)
    centered = values - mean
    var = jnp.sum(centered * centered, axis=0, keepdims=True) * (1.0 / 128.0)
    return (centered * lax.rsqrt(var + EPS) * gain).astype(BF16)


def nn(a, b):
    return lax.dot_general(a, b, (((1,), (0,)), ((), ())), preferred_element_type=F32)


def nt(a, b):
    return lax.dot_general(a, b, (((1,), (1,)), ((), ())), preferred_element_type=F32)


def tn(a, b):
    return lax.dot_general(a, b, (((0,), (0,)), ((), ())), preferred_element_type=F32)


def swap_lanes(blocks):
    blocks = list(blocks)
    lane = lax.broadcasted_iota(jnp.int32, blocks[0].shape, 1)
    for k in (4, 2, 1):
        low = (lane & (16 * k)) == 0
        for p in range(8):
            if p & k == 0:
                a, b = blocks[p], blocks[p | k]
                blocks[p] = jnp.where(low, a, pltpu.roll(b, 16 * k, 1))
                blocks[p | k] = jnp.where(low, pltpu.roll(a, 128 - 16 * k, 1), b)
    return blocks


def loop(n, body, start=0):
    def step(i, carry):
        body(i)
        return carry

    lax.fori_loop(start, n, step, 0)


def wait_bytes(ref, sem):
    pltpu.make_async_copy(ref, ref, sem).wait()


def kernel(
    x_ref, mask_ref, win_ref, wgate_ref, wout_ref, gin_ref, gout_ref, out_ref,
    xbuf, zt, normed, gate, maskv, wproj, wg, wo, gains,
    asend, arecv, bsend, brecv, rsend, rmid, tsend, trecv, rmat, rpair, lpair, lturn, cbuf, crecv, dsend, drecv,
    stage, stage_mid, stage_back, tile_sem, send_sem, recv_sem,
):
    r = lax.axis_index("row")
    c = lax.axis_index("col")
    core = r % 2
    rb = r // 2
    z = c % 8
    xl = c // 8

    zs = [(z + d) % 8 for d in range(8)]
    xs = [xl * 8, (1 - xl) * 8]
    ys = [(rb // 2 + d) % 4 * 2 for d in range(4)]
    hs = [rb % 2, 1 - rb % 2]

    def col_peer(n):
        hop = n // 2
        away = (hop + 1) // 2 * (1 - 2 * (hop % 2))
        return xs[n % 2] + zs[away % 8]

    def row_peer(n):
        return ys[n // 2] + hs[n % 2]

    def unrolled(n, body):
        for i in range(1, n):
            body(i)

    barrier = pltpu.get_barrier_semaphore()

    def greet(row, col):
        pl.semaphore_signal(barrier, inc=1, device_id=(row, col), device_id_type=MESH)

    unrolled(16, lambda n: greet(r, col_peer(n)))
    unrolled(8, lambda n: greet(row_peer(n) * 2 + core, c))
    greet(rb * 2 + 1 - core, c)

    def remote(src, dst, u, phase, q, row, col):
        return pltpu.make_async_remote_copy(
            src_ref=src, dst_ref=dst,
            send_sem=send_sem.at[u, phase, q], recv_sem=recv_sem.at[u, phase, q],
            device_id=(row, col), device_id_type=MESH,
        )

    tile_copies = [
        pltpu.make_async_copy(x_ref.at[pl.ds(q * 16, 16)], xbuf.at[pl.ds(q * 16, 16)], tile_sem.at[q]) for q in range(3)
    ]
    for copy in tile_copies:
        copy.start()

    def prepare_in(u):
        for t in range(4):
            turned = win_ref[u, t].astype(F32).T
            if t < 2:
                wproj[u, t] = turned.astype(BF16)
            else:
                stage[t] = turned
                for g in range(8):
                    wproj[u, t, g * 16 : g * 16 + 16] = stage[t, pl.ds(g, 16, stride=8), :].astype(BF16)
        gains[u, 0] = jnp.broadcast_to(gin_ref[u : u + 1, :], (128, 128)).T

    def prepare_rest(u):
        wg[u] = wgate_ref[u].astype(F32).T.astype(BF16)
        wo[u] = wout_ref[u].astype(F32).T.astype(BF16)
        gains[u, 1] = jnp.broadcast_to(gout_ref[u : u + 1, :], (128, 128)).T

    prepare_in(0)
    mask_row = jnp.broadcast_to(mask_ref[...].astype(F32)[None, :], (8, 768))
    row_part = pltpu.roll(mask_row, (768 - r * 48) % 768, 1)[:, :128].astype(BF16)
    col_part = pltpu.roll(mask_row, (768 - c * 48) % 768, 1)[:, :128].astype(BF16)
    place = lax.broadcasted_iota(jnp.int32, (128, 128), 0)
    lane = lax.broadcasted_iota(jnp.int32, (128, 128), 1)
    col_masks = [nn(col_part, (place == kh * 16 + (lane & 15)).astype(F32).astype(BF16)) for kh in range(3)]

    def load_rows(q):
        tile_copies[q].wait()
        for ih in range(2):
            ihg = q * 2 + ih
            rows = nn(row_part, (place == ihg * 8 + (lane >> 4)).astype(F32).astype(BF16))
            for kh in range(3):
                maskv[q * 3 + kh, ih] = rows * col_masks[kh]
                block = xbuf[ihg * 8 : ihg * 8 + 8, kh * 16 : kh * 16 + 16, :].reshape(128, 128)
                zt[q * 3 + kh, ih] = block.astype(F32).T

    def load_zt(i):
        return jnp.concatenate([zt[i, 0], zt[i, 1]], axis=1)

    def wide(block):
        return jnp.concatenate([block, block], axis=1)

    def project(u, q, kh, values):
        i = q * 3 + kh
        nrm = norm_rows(values, wide(gains[u, 0]))
        normed[i] = nrm
        mask = jnp.concatenate([maskv[i, 0], maskv[i, 1]], axis=1)[0:1]
        chunk, inner = (q, kh) if u == 0 else (kh, q)
        for side in (1, 0):
            for h in range(2):
                val = nn(wproj[u, 2 * side, h * 64 : h * 64 + 64], nrm)
                gat = nn(wproj[u, 2 * side + 1, h * 64 : h * 64 + 64], nrm)
                y = val * sigmoid(gat) * mask
                if side == 0:
                    y = y.reshape(8, 8, 256)
                    y = jnp.concatenate([y[:, :, :128], y[:, :, 128:]], axis=1).astype(BF16)
                    asend[u, chunk, h * 8 : h * 8 + 8, inner] = y
                else:
                    for ih in range(2):
                        part = y[:, ih * 128 : ih * 128 + 128].astype(BF16).reshape(4, 16, 128)
                        rsend[u, chunk, h * 4 : h * 4 + 4, inner, ih] = part

    def send_left(u, chunk):
        def one(n):
            s = col_peer(n)
            remote(asend.at[u, chunk, s], arecv.at[u, chunk, c], u, COLS_OUT, chunk, r, s).start()

        unrolled(16, one)
        arecv[u, chunk, c] = asend[u, chunk, c]

    def send_right(u, chunk):
        def one(n):
            peer = row_peer(n)
            remote(
                rsend.at[u, chunk, peer], rmid.at[u, chunk, rb], u, RIGHT_ROWS, chunk, peer * 2 + core, c
            ).start()

        unrolled(8, one)
        rmid[u, chunk, rb] = rsend[u, chunk, rb]

    def send_chunk(u, chunk):
        send_right(u, chunk)
        if chunk < AHEAD:
            send_left(u, chunk)

    def gates(u):
        def one(i):
            gate[i] = sigmoid(nn(wg[u], normed[i]))

        loop(9, one)

    def left_out(u, chunk):
        wait_bytes(arecv.at[u, chunk, pl.ds(0, 15)], recv_sem.at[u, COLS_OUT, chunk])

        def one(m):
            ch, inner = m // 3, m % 3
            parts = swap_lanes([arecv[u, chunk, 2 * p + ch, inner].astype(F32) for p in range(8)])
            for il in range(8):
                for ih in range(2):
                    stage[m, pl.ds(ih * 8 + il, 8, stride=16), :] = parts[il][ih * 8 : ih * 8 + 8]

        for m in range(6):
            one(m)

        def pack(d):
            bsend[u, chunk, d] = stage[:, d * 16 : d * 16 + 16, :].astype(BF16)

        for d in range(8):
            pack(d)

        def one_send(n):
            peer = row_peer(n)
            remote(
                bsend.at[u, chunk, peer], brecv.at[u, chunk, rb], u, ROWS_OUT, chunk, peer * 2 + core, c
            ).start()

        unrolled(8, one_send)
        brecv[u, chunk, rb] = bsend[u, chunk, rb]

    def left_copy(chunk):
        part = brecv.at[1, chunk, :, pl.ds((1 - core) * 3, 3)]
        return remote(part, lpair.at[chunk], 1, PAIR, 3 + chunk, rb * 2 + 1 - core, c)

    def left_take(u, chunk):
        wait_bytes(brecv.at[u, chunk, pl.ds(0, 7)], recv_sem.at[u, ROWS_OUT, chunk])
        if u == 1:
            left_copy(chunk).start()

    def left_turn(u, chunk):
        if u == 1:
            left_copy(chunk).wait_recv()
            for k in range(3):
                mine = brecv[u, chunk, :, core * 3 + k].reshape(128, 128)
                theirs = lpair[chunk, :, k].reshape(128, 128)
                lturn[chunk, 0, :, k * 128 : k * 128 + 128] = mine.astype(F32).T.astype(BF16)
                lturn[chunk, 1, :, k * 128 : k * 128 + 128] = theirs.astype(F32).T.astype(BF16)

    def right_mid(u, chunk):
        wait_bytes(rmid.at[u, chunk, pl.ds(0, 7)], recv_sem.at[u, RIGHT_ROWS, chunk])

        def one(inner):
            for g in range(8):
                for ih in range(2):
                    at = (g * 2 + ih) * 16
                    stage_mid[inner, at : at + 16, :] = rmid[u, chunk, g, inner, ih].astype(F32)
            for s in range(16):
                tsend[u, chunk, s, inner] = stage_mid[inner, pl.ds(s, 16, stride=16), :].astype(BF16)

        for inner in range(3):
            one(inner)

        def one_send(n):
            s = col_peer(n)
            remote(tsend.at[u, chunk, s], trecv.at[u, chunk, c], u, RIGHT_COLS, chunk, r, s).start()

        unrolled(16, one_send)
        trecv[u, chunk, c] = tsend[u, chunk, c]

    def right_copy(u, chunk):
        return remote(rmat.at[u, chunk], rpair.at[u, chunk], u, PAIR, chunk, rb * 2 + 1 - core, c)

    def right_in(u, chunk):
        wait_bytes(trecv.at[u, chunk, pl.ds(0, 15)], recv_sem.at[u, RIGHT_COLS, chunk])

        def one(m):
            ch, inner = m // 3, m % 3
            parts = swap_lanes([trecv[u, chunk, 2 * p + ch, inner].astype(F32) for p in range(8)])
            for il in range(8):
                stage[m, pl.ds(il, 16, stride=8), :] = parts[il]
            rmat[u, chunk, m] = stage[m].astype(BF16)

        for m in range(6):
            one(m)
        right_copy(u, chunk).start()

    def product(u, n):
        qi, jh = BLOCKS[n]
        if u == 0:
            left = jnp.concatenate([brecv[u, qi, :, m].reshape(128, 128) for m in range(6)], axis=1)
            mine = jnp.concatenate([rmat[u, jh, m] for m in range(6)], axis=1)
            theirs = jnp.concatenate([rpair[u, jh, m] for m in range(6)], axis=1)
            both = nt(left, jnp.concatenate([mine, theirs], axis=0)).astype(BF16)
            places = (core, 1 - core)
        else:
            mine = jnp.concatenate(
                [rmat[u, jh, 3 * k : 3 * k + 3].reshape(384, 128) for k in range(2)], axis=1
            )
            theirs = jnp.concatenate(
                [rpair[u, jh, 3 * k : 3 * k + 3].reshape(384, 128) for k in range(2)], axis=1
            )
            both = (nn(lturn[qi, 0], mine) + nn(lturn[qi, 1], theirs)).astype(BF16)
            places = (0, 1)
        for k in range(2):
            cbuf[u, :, n, places[k]] = both[:, k * 128 : k * 128 + 128].reshape(8, 16, 128)

    def products(u, w):
        begin, end = WAVES[w]
        for n in range(begin, end):
            product(u, n)
        span = pl.ds(begin, end - begin)

        def one(n):
            peer = row_peer(n)
            remote(
                cbuf.at[u, peer, span], crecv.at[u, rb, span], u, ROWS_BACK, w, peer * 2 + core, c
            ).start()

        unrolled(8, one)
        crecv[u, rb, span] = cbuf[u, rb, span]

    def regroup_back(u, w):
        begin, end = WAVES[w]
        size = end - begin
        span = pl.ds(begin, size)
        wait_bytes(crecv.at[u, pl.ds(0, 7), span], recv_sem.at[u, ROWS_BACK, w])

        def unpack(d):
            stage_back[0:size, :, d * 16 : d * 16 + 16, :] = crecv[u, d, span].astype(F32)

        for d in range(8):
            unpack(d)

        def one(n):
            for ch in range(2):
                rows = [
                    jnp.concatenate(
                        [stage_back[n, ch, pl.ds(ih * 8 + il, 8, stride=16), :] for ih in range(2)], axis=0
                    )
                    for il in range(8)
                ]
                for p, part in enumerate(swap_lanes(rows)):
                    dsend[u, 2 * p + ch, begin + n] = part.astype(BF16)

        for n in range(size):
            one(n)

        def one_send(n):
            s = col_peer(n)
            remote(dsend.at[u, s, span], drecv.at[u, c, span], u, COLS_BACK, w, r, s).start()

        unrolled(16, one_send)
        drecv[u, c, span] = dsend[u, c, span]

    def arrive_back(u, w):
        begin, end = WAVES[w]
        wait_bytes(drecv.at[u, pl.ds(0, 15), pl.ds(begin, end - begin)], recv_sem.at[u, COLS_BACK, w])

    def finish(u, n):
        q, kh = BLOCKS[n]
        i = q * 3 + kh
        got = drecv[u, :, n].astype(F32).reshape(16, 2, 8, 128)
        mixed = jnp.concatenate([got[:, 0].reshape(128, 128), got[:, 1].reshape(128, 128)], axis=1)
        branch = nn(wo[u], norm_rows(mixed, wide(gains[u, 1])))
        new = (load_zt(i) + gate[i] * branch).astype(BF16).astype(F32)
        for ih in range(2):
            half = new[:, ih * 128 : ih * 128 + 128]
            if u == 0:
                zt[i, ih] = half
            else:
                rows = (q * 2 + ih) * 8
                out_ref[rows : rows + 8, kh * 16 : kh * 16 + 16, :] = half.T.astype(BF16).reshape(8, 16, 128)
        if u == 0:
            project(1, q, kh, new)

    def first(q):
        load_rows(q)
        loop(3, lambda kh: project(0, q, kh, load_zt(q * 3 + kh)))

    first(0)
    pl.semaphore_wait(barrier, 23)
    send_chunk(0, 0)
    for q in (1, 2):
        first(q)
        send_chunk(0, q)
    prepare_in(1)
    for u in range(2):
        prepare_rest(u)
    steps = {
        "left": send_left, "gates": lambda u, index: gates(u), "out": left_out, "take": left_take, "turn": left_turn, "mid": right_mid, "in": right_in,
        "pair": lambda u, chunk: right_copy(u, chunk).wait_recv(), "product": products, "back": regroup_back,
        "land": arrive_back, "finish": finish, "next": lambda u, chunk: send_chunk(1, chunk) if u == 0 else None,
    }
    for u in range(2):
        for step, index in PLAN:
            steps[step](u, index)

    for u in range(2):
        for chunk in range(3):
            wait_bytes(asend.at[u, chunk, pl.ds(0, 15)], send_sem.at[u, COLS_OUT, chunk])
            wait_bytes(bsend.at[u, chunk, pl.ds(0, 7)], send_sem.at[u, ROWS_OUT, chunk])
            wait_bytes(rsend.at[u, chunk, pl.ds(0, 7)], send_sem.at[u, RIGHT_ROWS, chunk])
            wait_bytes(tsend.at[u, chunk, pl.ds(0, 15)], send_sem.at[u, RIGHT_COLS, chunk])
            right_copy(u, chunk).wait_send()
            if u == 1:
                left_copy(chunk).wait_send()
        for w, (begin, end) in enumerate(WAVES):
            span = pl.ds(begin, end - begin)
            wait_bytes(cbuf.at[u, pl.ds(0, 7), span], send_sem.at[u, ROWS_BACK, w])
            wait_bytes(dsend.at[u, pl.ds(0, 15), span], send_sem.at[u, COLS_BACK, w])


def body(pair_state, residue_mask, weight_in, weight_gate, weight_out, gain_in, gain_out):
    vmem = pl.BlockSpec(memory_space=pltpu.VMEM)
    weights = weight_in.transpose(0, 2, 1, 3)
    mask = residue_mask
    return pl.pallas_call(
        kernel,
        out_shape=jax.ShapeDtypeStruct((48, 48, 128), BF16),
        in_specs=[pl.BlockSpec(memory_space=pl.ANY)] + [vmem] * 6,
        out_specs=vmem,
        scratch_shapes=[
            pltpu.VMEM((48, 48, 128), BF16),
            pltpu.VMEM((9, 2, 128, 128), F32),
            pltpu.VMEM((9, 128, 256), BF16),
            pltpu.VMEM((9, 128, 256), F32),
            pltpu.VMEM((9, 2, 8, 128), F32),
            pltpu.VMEM((2, 4, 128, 128), BF16),
            pltpu.VMEM((2, 128, 128), BF16),
            pltpu.VMEM((2, 128, 128), BF16),
            pltpu.VMEM((2, 2, 128, 128), F32),
            pltpu.VMEM((2, 3, 16, 3, 16, 128), BF16),
            pltpu.VMEM((2, 3, 16, 3, 16, 128), BF16),
            pltpu.VMEM((2, 3, 8, 6, 16, 128), BF16),
            pltpu.VMEM((2, 3, 8, 6, 16, 128), BF16),
            pltpu.VMEM((2, 3, 8, 3, 2, 16, 128), BF16),
            pltpu.VMEM((2, 3, 8, 3, 2, 16, 128), BF16),
            pltpu.VMEM((2, 3, 16, 3, 16, 128), BF16),
            pltpu.VMEM((2, 3, 16, 3, 16, 128), BF16),
            pltpu.VMEM((2, 3, 6, 128, 128), BF16),
            pltpu.VMEM((2, 3, 6, 128, 128), BF16),
            pltpu.VMEM((3, 8, 3, 16, 128), BF16),
            pltpu.VMEM((3, 2, 128, 384), BF16),
            pltpu.VMEM((2, 8, 9, 2, 16, 128), BF16),
            pltpu.VMEM((2, 8, 9, 2, 16, 128), BF16),
            pltpu.VMEM((2, 16, 9, 16, 128), BF16),
            pltpu.VMEM((2, 16, 9, 16, 128), BF16),
            pltpu.VMEM((6, 128, 128), F32),
            pltpu.VMEM((3, 256, 128), F32),
            pltpu.VMEM((3, 2, 128, 128), F32),
            pltpu.SemaphoreType.DMA((3,)),
            pltpu.SemaphoreType.DMA((2, 7, 6)),
            pltpu.SemaphoreType.DMA((2, 7, 6)),
        ],
        compiler_params=pltpu.CompilerParams(
            collective_id=0, has_side_effects=True, vmem_limit_bytes=48 * 1024 * 1024
        ),
        name="triangle",
    )(pair_state, mask, weights, weight_gate, weight_out, gain_in, gain_out)


def solution(mesh):
    return jax.shard_map(
        body,
        mesh=mesh,
        in_specs=(P("row", "col", None), P(), P(), P(), P(), P(), P()),
        out_specs=P("row", "col", None),
        check_vma=False,
    )
```

time: 126 us -> 117 us (0.929); the launches traced: 126 us -> 115 us
  Pallas kernels: 122 us -> 111 us
    pallas_call x1, Pallas kernels: 122 us -> 111 us  [body(): pl.pallas_call(kernel, out_shape=jax.ShapeDtypeStruct((48, 48, 128), BF16...]
    unnamed x12 -> x14, local copies, waits for them, and re-layouts: 3.56 us -> 3.55 us
where the time goes in v2:
time: 117 us; the launch traced here: 115 us
  Pallas kernels  111 us (95%)
  local copies, waits for them, and re-layouts  3.55 us (3%)
    pallas_call x1, Pallas kernels, body(): pl.pallas_call(kernel, out_shape=jax.ShapeDtypeStruct((48, 48, 128), BF16...  111 us
    unnamed x14, local copies, waits for them, and re-layouts  3.55 us

profile of v2, /device:TPU:1, one launch (start us, length us, event | category | flops | bytes accessed | tf_op | source)
XLA Modules:
  0.0 114.8 jit_solution(10491372580893130938)
XLA Ops:
  0.0 0.0 copy-start.2
  0.0 0.0 copy-start.1
  0.0 0.0 copy-start.3
  0.0 0.0 copy-start.5
  0.0 1.0 copy.10
  1.0 0.0 copy-start.4
  1.1 0.0 copy-done.2
  1.1 0.0 copy-done.1
  1.1 0.0 copy-done.3
  1.1 0.0 copy-done.5
  1.1 0.6 copy-done.4
  1.7 0.0 copy-start
  1.7 1.1 copy-done
  2.8 111.2 %triangle.1 = bf16[48,48,128]{2,1,0:T(8,128)(2,1)S(1)} custom-call(bf16[48,48,128]{2,1,0:T(8,128)(2,1)S(1)} %copy-done, s32[768]{0:T(1024)S(1)} %copy-done.3, bf16[2,4,128,128]{3,2,1,0:T(8,128)(2,1)S(1)} %bitcast.3, bf16[2,128,128]{2,1,0:T(8,128)(2,1)S(1)} %copy-done.1, bf16[2,128,128]{2,1,0:T(8,128)(2,1)S(1)} %copy-done.2, f32[2,128]{1,0:T(2,128)S(1)} %copy-done.4, ...), custom_call_target="tpu_custom_call" | custom-call | tf_op jit(solution)/shard_map/triangle/pallas_call | solution.py:424
  114.0 0.8 copy.12
Async XLA Ops:
  0.0 1.1 copy-start.2
  0.0 1.1 copy-start.1
  0.0 1.1 copy-start.3
  0.0 1.1 copy-start.5
  1.0 0.7 copy-start.4
  1.7 1.1 copy-start

commit v3 on v2

--- a/solution.py
+++ b/solution.py
@@ -12,9 +12,9 @@
 COLS_OUT, ROWS_OUT, PAIR, ROWS_BACK, COLS_BACK, RIGHT_ROWS, RIGHT_COLS = range(7)
 AHEAD = 2
 BLOCKS = ((0, 0), (1, 0), (2, 0), (0, 1), (1, 1), (2, 1), (0, 2), (1, 2), (2, 2))
-WAVES = ((0, 2), (2, 3), (3, 6), (6, 9))
+WAVES = ((0, 2), (2, 3), (3, 6), (6, 7), (7, 9))
 PLAN = (
-    ("out", 0), ("left", 2), ("mid", 0), ("out", 1), ("mid", 1), ("out", 2), ("take", 0), ("take", 1), ("in", 0), ("mid", 2), ("gates", 0), ("turn", 0), ("turn", 1), ("take", 2), ("pair", 0), ("product", 0), ("turn", 2), ("product", 1), ("in", 1), ("back", 0), ("back", 1), ("pair", 1), ("product", 2), ("in", 2), ("land", 0), ("finish", 0), ("finish", 1), ("pair", 2), ("product", 3), ("back", 2), ("land", 1), ("finish", 2), ("next", 0), ("back", 3), ("land", 2), ("finish", 3), ("finish", 4), ("finish", 5), ("next", 1), ("land", 3), ("finish", 6), ("finish", 7), ("finish", 8), ("next", 2),
+    ("out", 0), ("left", 2), ("mid", 0), ("out", 1), ("mid", 1), ("out", 2), ("take", 0), ("take", 1), ("in", 0), ("mid", 2), ("gates", 0), ("turn", 0), ("turn", 1), ("take", 2), ("pair", 0), ("product", 0), ("turn", 2), ("product", 1), ("in", 1), ("back", 0), ("back", 1), ("pair", 1), ("product", 2), ("in", 2), ("land", 0), ("finish", 0), ("finish", 1), ("pair", 2), ("product", 3), ("product", 4), ("back", 2), ("land", 1), ("finish", 2), ("next", 0), ("back", 3), ("back", 4), ("land", 2), ("finish", 3), ("finish", 4), ("finish", 5), ("next", 1), ("land", 3), ("finish", 6), ("land", 4), ("finish", 7), ("finish", 8), ("next", 2),
 )
 
 
@@ -93,7 +93,7 @@
         return ys[n // 2] + hs[n % 2]
 
     def unrolled(n, body):
-        for i in range(1, n):
+        for i in range(n - 1, 0, -1):
             body(i)
 
     barrier = pltpu.get_barrier_semaphore()

time: 117 us -> 113 us (0.966)
  Pallas kernels: 111 us -> 107 us
    pallas_call x1, Pallas kernels: 111 us -> 107 us  [body(): pl.pallas_call(kernel, out_shape=jax.ShapeDtypeStruct((48, 48, 128), BF16...]
where the time goes in v3:
time: 113 us; the launch traced here: 111 us
  Pallas kernels  107 us (95%)
  local copies, waits for them, and re-layouts  3.55 us (3%)
    pallas_call x1, Pallas kernels, body(): pl.pallas_call(kernel, out_shape=jax.ShapeDtypeStruct((48, 48, 128), BF16...  107 us
    unnamed x14, local copies, waits for them, and re-layouts  3.55 us

profile of v3, /device:TPU:1, one launch (start us, length us, event | category | flops | bytes accessed | tf_op | source)
XLA Modules:
  0.0 111.0 jit_solution(11320731527097682283)
XLA Ops:
  0.0 0.0 copy-start.2
  0.0 0.0 copy-start.1
  0.0 0.0 copy-start.3
  0.0 0.0 copy-start.5
  0.0 1.0 copy.10
  1.0 0.0 copy-start.4
  1.1 0.0 copy-done.2
  1.1 0.0 copy-done.1
  1.1 0.0 copy-done.3
  1.1 0.0 copy-done.5
  1.1 0.6 copy-done.4
  1.7 0.0 copy-start
  1.7 1.1 copy-done
  2.8 107.3 %triangle.1 = bf16[48,48,128]{2,1,0:T(8,128)(2,1)S(1)} custom-call(bf16[48,48,128]{2,1,0:T(8,128)(2,1)S(1)} %copy-done, s32[768]{0:T(1024)S(1)} %copy-done.3, bf16[2,4,128,128]{3,2,1,0:T(8,128)(2,1)S(1)} %bitcast.3, bf16[2,128,128]{2,1,0:T(8,128)(2,1)S(1)} %copy-done.1, bf16[2,128,128]{2,1,0:T(8,128)(2,1)S(1)} %copy-done.2, f32[2,128]{1,0:T(2,128)S(1)} %copy-done.4, ...), custom_call_target="tpu_custom_call" | custom-call | tf_op jit(solution)/shard_map/triangle/pallas_call | solution.py:424
  110.1 0.8 copy.12
Async XLA Ops:
  0.0 1.1 copy-start.2
  0.0 1.1 copy-start.1
  0.0 1.1 copy-start.3
  0.0 1.1 copy-start.5
  1.0 0.7 copy-start.4
  1.7 1.1 copy-start
